TPU v7x, 32 devices: a whole 2x2x4 slice. The times are simulated.
32 devices in a mesh: gx: 8 (over y, x, core), gz: 4 (over z).
Axes of the slice: x: 2, y: 2, z: 4, core: 2. Of those that a mesh axis runs over, the one named last changes fastest.
Arguments:
- velocity: bfloat16 [2, 128, 2, 192, 512], P(None, None, None, 'gx', 'gz'), may hold values from -8 to 8
- snapshot_rank: int32 [128], replicated, may hold values from 0 to 127, each once
- anchor_index: int32 [64], replicated, may hold values from 0 to 196607
- start_basis: float32 [128, 64], replicated, may hold values from -6 to 6
Outputs:
- modes: bfloat16 [64, 2, 192, 512], P(None, None, 'gx', 'gz')
- basis: float32 [128, 64], replicated
All inputs are finite; a program needn't handle non-finite values.
Results may differ from a plain program's by a relative error of at most 0.0073.
Values may be sent and summed in bfloat16 or wider, within the bound.
A program may use at most 64 MiB of HBM per device.

v0:
```python
import jax
import jax.numpy as jnp
from jax import lax
from jax.sharding import PartitionSpec as P

ITERS = 3


def extended(cells, sides, width):
    for axis, dim in sides:
        count = lax.axis_size(axis)
        head = lax.slice_in_dim(cells, 0, width, axis=dim)
        tail = lax.slice_in_dim(cells, cells.shape[dim] - width, cells.shape[dim], axis=dim)
        cells = jnp.concatenate(
            [
                lax.ppermute(tail, axis, [(i, (i + 1) % count) for i in range(count)]),
                cells,
                lax.ppermute(head, axis, [((i + 1) % count, i) for i in range(count)]),
            ],
            axis=dim,
        )
    return cells


def orthonormal(block):
    inner = jnp.dot(block.T, block, precision=lax.Precision.HIGHEST)
    lower = jnp.linalg.cholesky(inner)
    return jax.scipy.linalg.solve_triangular(lower, block.T, lower=True).T


def body(velocity, snapshot_rank, anchor_index, start_basis):
    snaps = velocity.shape[1]
    planes = velocity.shape[2]
    cols_x = velocity.shape[3]
    cols_z = velocity.shape[4]
    kept = start_basis.shape[1]
    wide_w = extended(velocity[1], (("gx", 2),), 3)
    wide_u = extended(velocity[0], (("gz", 3),), 3)
    weights = (45.0 / 60.0, -9.0 / 60.0, 1.0 / 60.0)
    total = jnp.zeros((snaps, planes, cols_x, cols_z), jnp.float32)
    for shift_by in range(1, 4):
        weight_now = weights[shift_by - 1]
        ahead_w = wide_w[:, :, 3 + shift_by : 3 + shift_by + cols_x, :].astype(jnp.float32)
        behind_w = wide_w[:, :, 3 - shift_by : 3 - shift_by + cols_x, :].astype(jnp.float32)
        ahead_u = wide_u[:, :, :, 3 + shift_by : 3 + shift_by + cols_z].astype(jnp.float32)
        behind_u = wide_u[:, :, :, 3 - shift_by : 3 - shift_by + cols_z].astype(jnp.float32)
        total = total + weight_now * (ahead_w - behind_w) - weight_now * (ahead_u - behind_u)
    flat = total.astype(jnp.bfloat16).reshape(snaps, planes * cols_x * cols_z)
    local_gram = lax.dot_general(
        flat, flat, (((1,), (1,)), ((), ())), preferred_element_type=jnp.float32
    )
    gram = lax.psum(local_gram, ("gx", "gz"))
    count_x = lax.axis_size("gx")
    count_z = lax.axis_size("gz")
    total_x = cols_x * count_x
    total_z = cols_z * count_z
    gram = gram / float(planes * total_x * total_z)
    scale = jnp.where(snapshot_rank < kept, 1.0, 0.25).astype(jnp.float32)
    weighted = scale[:, None] * gram * scale[None, :]
    basis_now = start_basis
    for step in range(ITERS):
        basis_now = orthonormal(jnp.dot(weighted, basis_now, precision=lax.Precision.HIGHEST))
    coef = (scale[:, None] * basis_now).astype(jnp.bfloat16)
    raw = lax.dot_general(coef, flat, (((0,), (0,)), ((), ())), preferred_element_type=jnp.float32)
    plane_of = anchor_index // (total_x * total_z)
    remain = anchor_index % (total_x * total_z)
    local_x = remain // total_z - lax.axis_index("gx") * cols_x
    local_z = remain % total_z - lax.axis_index("gz") * cols_z
    owned = (local_x >= 0) & (local_x < cols_x) & (local_z >= 0) & (local_z < cols_z)
    position = (plane_of * cols_x + jnp.clip(local_x, 0, cols_x - 1)) * cols_z + jnp.clip(
        local_z, 0, cols_z - 1
    )
    values = jnp.take_along_axis(raw, position[:, None], axis=1)[:, 0]
    term = jnp.where(owned, values, 0.0)
    anchor = lax.psum(term, ("gx", "gz"))
    orient = anchor / jnp.maximum(jnp.abs(anchor), 1.0)
    modes = (raw * orient[:, None]).astype(jnp.bfloat16).reshape(kept, planes, cols_x, cols_z)
    return (modes, basis_now * orient[None, :])


def solution(mesh):
    return jax.shard_map(
        body,
        mesh=mesh,
        in_specs=(P(None, None, None, "gx", "gz"), P(), P(), P()),
        out_specs=(P(None, None, "gx", "gz"), P()),
        check_vma=False,
    )
```

profile of v0, /device:TPU:0, one launch (start us, length us, event | category | flops | bytes accessed | tf_op | source)
XLA Modules:
  0.0 248.9 jit_solution(12989056838306947043)
XLA Ops:
  7.2 0.0 copy-start
  7.2 0.0 all-reduce.2.cloned.1.call-start
  7.2 3.6 %fusion.43 = (bf16[1,128,2,24,128]{4,3,2,1,0:T(8,128)(2,1)}, bf16[1,128,2,24,128]{4,3,2,1,0:T(8,128)(2,1)S(1)}) fusion(bf16[2,128,2,24,128]{4,3,2,1,0:T(8,128)(2,1)} %param.7), kind=kLoop, calls=%fused_computation.91 | loop fusion | bytes 6291456 | tf_op jit(solution)/shard_map/slice | solution.py:38
  10.8 0.0 copy-start.2
  10.8 0.0 copy-start.3
  10.8 1.1 copy.37
  11.9 0.8 fusion.44
  12.7 3.3 %collective-permute-start = (bf16[128,2,3,128]{0,3,2,1:T(8,128)(2,1)}, bf16[128,2,3,128]{0,3,2,1:T(8,128)(2,1)S(1)}, u32[]{:S(2)}, u32[]{:S(2)}) collective-permute-start(bf16[128,2,3,128]{0,3,2,1:T(8,128)(2,1)} %get-tuple-element.9), channel_id=1, source_target_pairs={{4,0},{8,4},{12,8},{16,12},{20,16},{24,20},{28,24},{0,28},{5,1},{9... | collective-permute-start | bytes 589832 | tf_op jit(solution)/shard_map/ppermute | solution.py:18
  16.0 0.0 collective-permute-start.1
  16.0 2.1 copy.38
  18.2 0.0 copy-start.1
  18.2 3.7 %collective-permute-start.2 = (bf16[128,2,24,3]{0,2,3,1:T(8,128)(2,1)S(1)}, bf16[128,2,24,3]{0,2,3,1:T(8,128)(2,1)S(1)}, u32[]{:S(2)}, u32[]{:S(2)}) collective-permute-start(bf16[128,2,24,3]{0,2,3,1:T(8,128)(2,1)S(1)} %copy.25), channel_id=1, source_target_pairs={{1,0},{2,1},{3,2},{0,3},{5,4},{6,5},{7,6},{4,7},{9,8},{10,9},{11,1... | collective-permute-start | bytes 110600 | tf_op jit(solution)/shard_map/ppermute | solution.py:18
  21.9 0.1 collective-permute-start.3
  22.0 0.0 copy-done.2
  22.0 0.0 copy-done.3
  22.1 1.5 collective-permute-done.2
  23.6 4.2 %collective-permute-done.3 = bf16[128,2,24,3]{0,2,3,1:T(8,128)(2,1)S(1)} collective-permute-done((bf16[128,2,24,3]{0,2,3,1:T(8,128)(2,1)S(1)}, bf16[128,2,24,3]{0,2,3,1:T(8,128)(2,1)S(1)}, u32[]{:S(2)}, u32[]{:S(2)}) %collective-permute-start.3) | collective-permute-done | bytes 36896 | tf_op jit(solution)/shard_map/ppermute | solution.py:16
  27.7 0.0 collective-permute-done
  27.8 0.0 copy-done.1
  27.8 0.0 collective-permute-done.1
  27.8 12.7 %subtract_convert_fusion = bf16[128,2,24,128]{0,3,2,1:T(8,128)(2,1)S(1)} fusion(bf16[128,2,24,128]{0,3,2,1:T(8,128)(2,1)S(1)} %bitcast.68, bf16[128,2,24,3]{0,3,2,1:T(4,128)(2,1)S(1)} %copy.28, bf16[128,2,24,3]{0,3,2,1:T(4,128)(2,1)S(1)} %copy.26, bf16[128,2,3,128]{0,3,2,1:T(8,128)(2,1)} %collective-permute-done.1, ...), kind=kLoop, calls=%fused_computation.1 | loop fusion | flops 51904512 | bytes 5185536 | tf_op jit(solution)/shard_map/convert_element_type | solution.py:48
  40.4 1.2 convolution_bitcast_fusion
  41.7 0.0 all-reduce.2.cloned.1.call-update
  41.7 114.7 %all-reduce.2.cloned.1.call-done = f32[128,128]{1,0:T(8,128)} async-done(((f32[128,128]{1,0:T(8,128)}), f32[128,128]{1,0:T(8,128)}) %all-reduce.2.cloned.1.call-update) | async-done | bytes 65552 | tf_op jit(solution)/shard_map/psum | solution.py:52
  156.4 0.0 copy-done
  156.4 1.1 fusion.11
  157.5 0.2 fusion.46
  157.7 0.1 copy.31
  157.8 5.8 %cholesky.59 = f32[64,64]{1,0:T(8,128)S(1)} custom-call(f32[64,64]{1,0:T(8,128)S(1)} %fusion.26), custom_call_target="Cholesky" | custom-call | tf_op jit(solution)/shard_map/jit(cholesky)/cholesky | solution.py:27
  163.7 0.6 compare_reduce_fusion.2
  164.3 0.7 fusion.12
  165.0 4.9 %custom-call.9 = f32[1,64,64]{1,2,0:T(8,128)S(1)} custom-call(f32[1,64,64]{2,1,0:T(8,128)S(1)} %fusion.12), custom_call_target="InvertDiagBlocksLowerTriangular" | custom-call | tf_op jit(solution)/shard_map/jit(_solve_triangular)/triangular_solve | solution.py:28
  169.9 0.3 fusion.23
  170.2 1.2 fusion.10
  171.3 0.2 fusion.47
  171.5 0.1 copy.32
  171.6 5.8 %cholesky.70 = f32[64,64]{1,0:T(8,128)S(1)} custom-call(f32[64,64]{1,0:T(8,128)S(1)} %fusion.22), custom_call_target="Cholesky" | custom-call | tf_op jit(solution)/shard_map/jit(cholesky)/cholesky | solution.py:27
  177.5 0.6 compare_reduce_fusion.1
  178.1 0.7 fusion.13
  178.8 4.9 %custom-call.10 = f32[1,64,64]{1,2,0:T(8,128)S(1)} custom-call(f32[1,64,64]{2,1,0:T(8,128)S(1)} %fusion.13), custom_call_target="InvertDiagBlocksLowerTriangular" | custom-call | tf_op jit(solution)/shard_map/jit(_solve_triangular)/triangular_solve | solution.py:28
  183.7 0.3 fusion.19
  183.9 1.2 fusion.9
  185.1 0.2 fusion.48
  185.3 0.1 copy.33
  185.4 5.8 %cholesky.81 = f32[64,64]{1,0:T(8,128)S(1)} custom-call(f32[64,64]{1,0:T(8,128)S(1)} %fusion.18), custom_call_target="Cholesky" | custom-call | tf_op jit(solution)/shard_map/jit(cholesky)/cholesky | solution.py:27
  191.3 0.6 compare_reduce_fusion
  191.9 0.7 fusion.14
  192.6 4.9 %custom-call.11 = f32[1,64,64]{1,2,0:T(8,128)S(1)} custom-call(f32[1,64,64]{2,1,0:T(8,128)S(1)} %fusion.14), custom_call_target="InvertDiagBlocksLowerTriangular" | custom-call | tf_op jit(solution)/shard_map/jit(_solve_triangular)/triangular_solve | solution.py:28
  197.5 0.3 fusion.15
  197.7 0.7 fusion.37
  198.4 0.9 gather_fusion
  199.3 40.9 %psum.15 = f32[64]{0:T(128)S(1)} all-reduce(f32[64]{0:T(128)S(1)} %and_select_fusion.2), channel_id=1, replica_groups=mesh['gx'=8,'gz'=4] {'gx','gz'}, use_global_device_ids=true, to_apply=%region_3.6 | all-reduce | flops 64 | bytes 512 | tf_op jit(solution)/shard_map/psum | solution.py:75
  240.2 0.7 multiply_bitcast_fusion
  240.9 0.2 fusion.8
  241.1 1.0 copy.39
  (18 shorter events, 0.3 us)
Async XLA Ops:
  7.2 149.2 %copy-start = (f32[128,64]{0,1:T(8,128)S(1)}, f32[128,64]{0,1:T(8,128)}, u32[]{:S(2)}) copy-start(f32[128,64]{0,1:T(8,128)} %param.10) | copy-start | bytes 98308
  7.2 149.2 %all-reduce.2.cloned.1.call-start = ((), (), s32[]{:S(2)}) async-start(), calls=%async_computation | async-start | bytes 131072 | tf_op jit(solution)/shard_map/psum | solution.py:52
  10.8 11.2 %copy-start.2 = (s32[64]{0:T(128)S(1)}, s32[64]{0:T(128)}, u32[]{:S(2)}) copy-start(s32[64]{0:T(128)} %param.9) | copy-start | bytes 772
  10.8 11.2 %copy-start.3 = (s32[128]{0:T(128)S(1)}, s32[128]{0:T(128)}, u32[]{:S(2)}) copy-start(s32[128]{0:T(128)} %param.8) | copy-start | bytes 1540
  12.7 15.0 %collective-permute-start = (bf16[128,2,3,128]{0,3,2,1:T(8,128)(2,1)}, bf16[128,2,3,128]{0,3,2,1:T(8,128)(2,1)S(1)}, u32[]{:S(2)}, u32[]{:S(2)}) collective-permute-start(bf16[128,2,3,128]{0,3,2,1:T(8,128)(2,1)} %get-tuple-element.9), channel_id=1, source_target_pairs={{4,0},{8,4},{12,8},{16,12},{20,16},{24,20},{28,24},{0,28},{5,1},{9... | collective-permute-start | bytes 589832 | tf_op jit(solution)/shard_map/ppermute | solution.py:18
  16.0 11.7 %collective-permute-start.1 = (bf16[128,2,3,128]{0,3,2,1:T(8,128)(2,1)}, bf16[128,2,3,128]{0,3,2,1:T(8,128)(2,1)}, u32[]{:S(2)}, u32[]{:S(2)}) collective-permute-start(bf16[128,2,3,128]{0,3,2,1:T(8,128)(2,1)} %get-tuple-element.10), channel_id=1, source_target_pairs={{0,4},{4,8},{8,12},{12,16},{16,20},{20,24},{24,28},{28,0},{1,5},{5... | collective-permute-start | bytes 589832 | tf_op jit(solution)/shard_map/ppermute | solution.py:16
  18.2 9.6 %copy-start.1 = (bf16[1,128,2,24,128]{1,4,3,2,0:T(8,128)(2,1)}, bf16[1,128,2,24,128]{1,4,3,2,0:T(8,128)(2,1)S(1)}, u32[]{:S(2)}) copy-start(bf16[1,128,2,24,128]{1,4,3,2,0:T(8,128)(2,1)S(1)} %copy.38) | copy-start | bytes 4718596
  18.2 5.3 %collective-permute-start.2 = (bf16[128,2,24,3]{0,2,3,1:T(8,128)(2,1)S(1)}, bf16[128,2,24,3]{0,2,3,1:T(8,128)(2,1)S(1)}, u32[]{:S(2)}, u32[]{:S(2)}) collective-permute-start(bf16[128,2,24,3]{0,2,3,1:T(8,128)(2,1)S(1)} %copy.25), channel_id=1, source_target_pairs={{1,0},{2,1},{3,2},{0,3},{5,4},{6,5},{7,6},{4,7},{9,8},{10,9},{11,1... | collective-permute-start | bytes 110600 | tf_op jit(solution)/shard_map/ppermute | solution.py:18
  21.9 5.8 %collective-permute-start.3 = (bf16[128,2,24,3]{0,2,3,1:T(8,128)(2,1)S(1)}, bf16[128,2,24,3]{0,2,3,1:T(8,128)(2,1)S(1)}, u32[]{:S(2)}, u32[]{:S(2)}) collective-permute-start(bf16[128,2,24,3]{0,2,3,1:T(8,128)(2,1)S(1)} %copy.27), channel_id=1, source_target_pairs={{0,1},{1,2},{2,3},{3,0},{4,5},{5,6},{6,7},{7,4},{8,9},{9,10},{10,1... | collective-permute-start | bytes 110600 | tf_op jit(solution)/shard_map/ppermute | solution.py:16
Sparse Core Ops, SparseCore 0:
  41.8 114.5 all-reduce.1
where the time goes:
time: 249 us
  waiting for transfers between devices  120 us (48%)
  other arithmetic  49.9 us (20%)
  blocking collectives  40.9 us (16%)
  between operations  14.3 us (6%)
  local copies, waits for them, and re-layouts  9.83 us (4%)
  starting transfers between devices  7.09 us (3%)
  matrix products  6.65 us (3%)
    psum x1, waiting for transfers between devices, body(): gram = lax.psum(local_gram, ('gx', 'gz'))  115 us
    psum x1, blocking collectives, body(): anchor = lax.psum(term, ('gx', 'gz'))  40.9 us
    another operation x9, other arithmetic, orthonormal(): lower = jnp.linalg.cholesky(inner)  19.6 us
    another operation x6, other arithmetic, orthonormal(): return jax.scipy.linalg.solve_triangular(lower, block.T, lower=True).T  16.6 us
    convert_element_type x1, other arithmetic, body(): flat = total.astype(jnp.bfloat16).reshape(snaps, planes * cols_x * cols_z)  12.7 us
    ppermute x2, starting transfers between devices, extended(): lax.ppermute(head, axis, [((i + 1) % count, i) for i in range(count)])  6.99 us
  transfers between devices with their start and end apart: 5, of which 3 were waited for; matrix products, arithmetic and copies ran while one was open for 1% of the time, Pallas kernels for 0%

commit v1 on v0

v1 whole, which is shorter than its diff:
```python
import functools
import jax
import jax.numpy as jnp
from jax import lax
from jax.experimental import pallas as pl
from jax.experimental.pallas import tpu as pltpu
from jax.sharding import PartitionSpec as P

ITERS = 3
REACH = 3
MESH = pl.DeviceIdType.MESH
NT = (((1,), (1,)), ((), ()))
F32 = jnp.float32
BF16 = jnp.bfloat16


def iota(shape, dim):
    return lax.broadcasted_iota(jnp.int32, shape, dim)


def stencil_weight(offset):
    size = jnp.abs(offset)
    value = jnp.where(size == 1, 45, jnp.where(size == 2, -9, jnp.where(size == 3, 1, 0)))
    return jnp.where(offset < 0, -value, value).astype(F32).astype(BF16)


def gram_kernel(
    dims, vel_ref, anchor_ref, flat_ref, out_ref,
    wide, uterm, sendx, recvx, sendz, recvz, part, got1, got2, got3,
    sx_sem, rx_sem, sz_sem, rz_sem, s1_sem, r1_sem, s2_sem, r2_sem, s3_sem, r3_sem, s4_sem, r4_sem,
):
    snaps, planes, cx, cz, kept, nx, nz, group = dims
    rows = snaps * planes * cx
    stride = planes * cx
    me_x = lax.axis_index("gx")
    me_z = lax.axis_index("gz")
    member = lax.rem(me_x, group)
    base = me_x - member
    teams = nx // group
    team = me_x // group
    share = part.shape[0] // group
    xnext, xprev = lax.rem(me_x + 1, nx), lax.rem(me_x + nx - 1, nx)
    znext, zprev = lax.rem(me_z + 1, nz), lax.rem(me_z + nz - 1, nz)

    in_group = [(base + lax.rem(member + d, group), me_z) for d in range(1, group)]
    in_teams = [(lax.rem(team + d, teams) * group + member, me_z) for d in range(1, teams)]
    in_z = [(me_x, lax.rem(me_z + d, nz)) for d in range(1, nz)]
    greet = in_group + in_teams + in_z
    if teams > 1:
        greet = greet + [(xnext, me_z), (xprev, me_z)]

    barrier = pltpu.get_barrier_semaphore()
    for peer in greet:
        pl.semaphore_signal(barrier, inc=1, device_id=peer, device_id_type=MESH)

    def remote(src, dst, send, recv, peer):
        return pltpu.make_async_remote_copy(
            src_ref=src, dst_ref=dst, send_sem=send, recv_sem=recv,
            device_id=peer, device_id_type=MESH,
        )

    quarter = rows // 4
    edge = iota((32, cz), 0)
    lane = iota((32, cz), 1)
    packed = jnp.zeros((32, quarter), F32)
    for c in range(4):
        r = edge % 16 - 4 * c
        wanted = jnp.where(edge < 16, cz - REACH + r, r)
        pick = jnp.where((r >= 0) & (r < REACH) & (lane == wanted), 1.0, 0.0).astype(BF16)
        packed = packed + lax.dot_general(
            pick, vel_ref[0, c * quarter : (c + 1) * quarter, :], NT, preferred_element_type=F32
        )
    sendz[...] = packed.astype(BF16).reshape(2, 16, quarter)

    wide[...] = vel_ref[1].astype(F32)
    for p in range(planes):
        for r in range(REACH):
            low = wide[pl.ds(p * cx + r, snaps, stride=stride), :]
            high = wide[pl.ds(p * cx + cx - REACH + r, snaps, stride=stride), :]
            sendx[0, p * REACH + r] = high.astype(BF16)
            sendx[1, p * REACH + r] = low.astype(BF16)

    pl.semaphore_wait(barrier, len(greet))
    halos = [
        remote(sendz.at[0], recvz.at[0], sz_sem.at[0], rz_sem.at[0], (me_x, znext)),
        remote(sendz.at[1], recvz.at[1], sz_sem.at[1], rz_sem.at[1], (me_x, zprev)),
        remote(sendx.at[0], recvx.at[0], sx_sem.at[0], rx_sem.at[0], (xnext, me_z)),
        remote(sendx.at[1], recvx.at[1], sx_sem.at[1], rx_sem.at[1], (xprev, me_z)),
    ]
    for copy in halos:
        copy.start()

    index = anchor_ref[...]
    total_x, total_z = cx * nx, cz * nz
    plane_of = index // (total_x * total_z)
    remain = index % (total_x * total_z)
    local_x = remain // total_z - me_x * cx
    local_z = remain % total_z - me_z * cz
    owned = (local_x >= 0) & (local_x < cx) & (local_z >= 0) & (local_z < cz)
    position = jnp.where(owned, (plane_of * cx + local_x) * cz + local_z, -1).astype(F32)
    column = jnp.transpose(jnp.broadcast_to(position, (kept, kept)))[:, 0:1]

    band = stencil_weight(iota((cz, cz), 1) - iota((cz, cz), 0))
    halos[0].wait_recv()
    halos[1].wait_recv()
    sides = jnp.transpose(recvz[...].reshape(32, quarter).astype(F32)).astype(BF16)
    for c in range(4):
        r = edge % 16 - 4 * c
        source = jnp.where(edge < 16, r - REACH, cz + r)
        valid = (r >= 0) & (r < REACH)
        spread = stencil_weight(jnp.where(valid, lane - source, 0))
        here = slice(c * quarter, (c + 1) * quarter)
        uterm[here, :] = jnp.dot(
            vel_ref[0, here, :], band, preferred_element_type=F32
        ) + jnp.dot(sides, spread, preferred_element_type=F32)
    halos[2].wait_recv()
    halos[3].wait_recv()

    def snapshots(step, carry):
        first = pl.multiple_of(step * 16, 16)
        for p in range(planes):
            layers = []
            for x in range(-REACH, cx + REACH):
                if x < 0:
                    block = recvx[0, p * REACH + x + REACH, pl.ds(first, 16), :].astype(F32)
                elif x >= cx:
                    block = recvx[1, p * REACH + x - cx, pl.ds(first, 16), :].astype(F32)
                else:
                    block = wide[pl.ds(first * stride + p * cx + x, 16, stride=stride), :]
                layers.append(block)
            for x in range(cx):
                at = x + REACH
                value = 45.0 * (layers[at + 1] - layers[at - 1])
                value = value - 9.0 * (layers[at + 2] - layers[at - 2])
                value = value + (layers[at + 3] - layers[at - 3])
                value = value + uterm[pl.ds(first * stride + p * cx + x, 16, stride=stride), :]
                cell = (p * cx + x) * cz
                flat_ref[pl.ds(first, 16), cell : cell + cz] = (value * (1.0 / 60.0)).astype(BF16)
        return carry

    lax.fori_loop(0, snaps // 16, snapshots, 0)

    width = 8 * cz
    cell_in = iota((kept, width), 1).astype(F32)

    def products(step, total):
        at = pl.multiple_of(step * width, width)
        block = flat_ref[:, pl.ds(at, width)]
        mark = jnp.where(cell_in + (step * width).astype(F32) == column, 1.0, 0.0).astype(BF16)
        both = jnp.concatenate([block, mark], axis=0)
        return total + lax.dot_general(both, block, NT, preferred_element_type=F32)

    part[...] = lax.fori_loop(
        0, planes * cx * cz // width, products, jnp.zeros((snaps + kept, snaps), F32)
    )

    started = list(halos)
    first_stage = []
    for d in range(1, group):
        target = lax.rem(member + d, group)
        first_stage.append(remote(
            part.at[pl.ds(target * share, share)], got1.at[d - 1],
            s1_sem.at[d - 1], r1_sem.at[d - 1], in_group[d - 1],
        ))
    for copy in first_stage:
        copy.start()
    mine = part[pl.ds(member * share, share), :]
    for d, copy in enumerate(first_stage):
        copy.wait_recv()
        mine = mine + got1[d]

    def exchange(value, buffer, place, peers, send, recv):
        buffer[place] = value
        copies = [
            remote(buffer.at[place], buffer.at[place], send.at[d], recv.at[d], peer)
            for d, peer in enumerate(peers)
        ]
        for copy in copies:
            copy.start()
        for copy in copies:
            copy.wait_recv()
        started.extend(copies)
        value = buffer[0]
        for other in range(1, len(peers) + 1):
            value = value + buffer[other]
        return value

    if teams > 1:
        mine = exchange(mine, got2, team, in_teams, s4_sem, r4_sem)
    mine = exchange(mine, got3, me_z, in_z, s2_sem, r2_sem)

    home = pl.ds(member * share, share)
    out_ref[home, :] = mine
    last_stage = [
        remote(out_ref.at[home], out_ref.at[home], s3_sem.at[d], r3_sem.at[d], peer)
        for d, peer in enumerate(in_group)
    ]
    for copy in last_stage:
        copy.start()
    for copy in last_stage:
        copy.wait_recv()
    for copy in started + first_stage + last_stage:
        copy.wait_send()


def orthonormal_rows(block, pivots):
    kept, snaps = block.shape
    inner = lax.dot_general(
        block, block, NT, precision=lax.Precision.HIGHEST, preferred_element_type=F32
    )
    groups = kept // 8
    left = [inner[8 * h : 8 * h + 8, :] for h in range(groups)]
    right = [block[8 * h : 8 * h + 8, :] for h in range(groups)]
    row_in = iota((8, snaps), 0)
    for k0 in range(0, kept, pivots):
        g = k0 // 8
        cols = [
            {h: jnp.broadcast_to(left[h][:, k0 + j : k0 + j + 1], (8, snaps)) for h in range(g, groups)}
            for j in range(pivots)
        ]
        for j in range(pivots):
            s = (k0 + j) % 8
            pivot = jnp.broadcast_to(cols[j][g][s : s + 1, :], (8, snaps))
            inverse = 1.0 / pivot
            root = inverse * jnp.sqrt(pivot)
            ahead = [cols[n][g][s : s + 1, :] * inverse for n in range(j + 1, pivots)]
            left_row = left[g][s : s + 1, :] * inverse[:, :kept]
            right_row = right[g][s : s + 1, :] * inverse
            for h in range(g, groups):
                factor = cols[j][h]
                if h == g:
                    factor = jnp.where(row_in > s, factor, 0.0)
                left[h] = left[h] - factor[:, :kept] * left_row
                right[h] = right[h] - factor * right_row
                for n in range(j + 1, pivots):
                    cols[n][h] = cols[n][h] - factor * ahead[n - j - 1]
            right[g] = jnp.where(row_in == s, right[g] * root, right[g])
    return jnp.concatenate(right, axis=0)


def modes_kernel(dims, gram_ref, flat_ref, rank_ref, start_ref, modes_ref, basis_ref, spread):
    snaps, planes, cx, cz, kept, nx, nz, group = dims
    cells = float(planes * cx * nx * cz * nz)
    stride = planes * cx
    scale = jnp.where(rank_ref[...] < kept, 1.0, 0.25).astype(F32)
    down = jnp.transpose(jnp.broadcast_to(scale, (snaps, snaps)))
    weighted = down * (gram_ref[0:snaps, :] / cells) * scale

    def iterate(step, rows):
        moved = lax.dot_general(
            rows, weighted, NT, precision=lax.Precision.HIGHEST, preferred_element_type=F32
        )
        return orthonormal_rows(moved, 4)

    rows = lax.fori_loop(0, ITERS, iterate, jnp.transpose(start_ref[...]))
    coef = (scale * rows).astype(BF16)
    anchor = jnp.sum(gram_ref[snaps : snaps + kept, :] * coef.astype(F32), axis=1, keepdims=True)
    orient = anchor / jnp.maximum(jnp.abs(anchor), 1.0)
    basis_ref[...] = jnp.transpose(rows * orient)
    for block in range(stride):
        raw = jnp.dot(
            coef, flat_ref[:, block * cz : (block + 1) * cz], preferred_element_type=F32
        )
        spread[pl.ds(block, kept, stride=stride), :] = raw * orient
    modes_ref[...] = spread[...].astype(BF16)


def body(nx, nz, velocity, snapshot_rank, anchor_index, start_basis):
    _, snaps, planes, cx, cz = velocity.shape
    kept = start_basis.shape[1]
    total = snaps + kept
    group = max(g for g in (1, 2, 4, 8, 3, 6, 12, 24) if nx % g == 0 and total % (8 * g) == 0)
    dims = (snaps, planes, cx, cz, kept, nx, nz, group)
    rows = snaps * planes * cx
    share = total // group
    teams = nx // group
    vmem = pl.BlockSpec(memory_space=pltpu.VMEM)
    dma = lambda n: pltpu.SemaphoreType.DMA((max(n, 1),))
    flat, gram = pl.pallas_call(
        functools.partial(gram_kernel, dims),
        out_shape=(
            jax.ShapeDtypeStruct((snaps, planes * cx * cz), BF16),
            jax.ShapeDtypeStruct((total, snaps), F32),
        ),
        in_specs=[vmem] * 2,
        out_specs=(vmem, vmem),
        scratch_shapes=[
            pltpu.VMEM((rows, cz), F32),
            pltpu.VMEM((rows, cz), F32),
            pltpu.VMEM((2, planes * REACH, snaps, cz), BF16),
            pltpu.VMEM((2, planes * REACH, snaps, cz), BF16),
            pltpu.VMEM((2, 16, rows // 4), BF16),
            pltpu.VMEM((2, 16, rows // 4), BF16),
            pltpu.VMEM((total, snaps), F32),
            pltpu.VMEM((max(group - 1, 1), share, snaps), F32),
            pltpu.VMEM((teams, share, snaps), F32),
            pltpu.VMEM((nz, share, snaps), F32),
            dma(2), dma(2), dma(2), dma(2),
            dma(group - 1), dma(group - 1),
            dma(nz - 1), dma(nz - 1),
            dma(group - 1), dma(group - 1),
            dma(teams - 1), dma(teams - 1),
        ],
        compiler_params=pltpu.CompilerParams(
            collective_id=0, has_side_effects=True, vmem_limit_bytes=40 * 1024 * 1024
        ),
        name="vorticity_gram",
    )(velocity.reshape(2, rows, cz), anchor_index.reshape(1, kept))
    modes, basis = pl.pallas_call(
        functools.partial(modes_kernel, dims),
        out_shape=(
            jax.ShapeDtypeStruct((kept * planes * cx, cz), BF16),
            jax.ShapeDtypeStruct((snaps, kept), F32),
        ),
        in_specs=[vmem] * 4,
        out_specs=(vmem, vmem),
        scratch_shapes=[pltpu.VMEM((kept * planes * cx, cz), F32)],
        compiler_params=pltpu.CompilerParams(vmem_limit_bytes=40 * 1024 * 1024),
        name="subspace_modes",
    )(gram, flat, snapshot_rank.reshape(1, snaps), start_basis)
    return modes.reshape(kept, planes, cx, cz), basis


def solution(mesh):
    return jax.shard_map(
        functools.partial(body, mesh.shape["gx"], mesh.shape["gz"]),
        mesh=mesh,
        in_specs=(P(None, None, None, "gx", "gz"), P(), P(), P()),
        out_specs=(P(None, None, "gx", "gz"), P()),
        check_vma=False,
    )
```

time: 249 us -> 42.2 us (0.17)
  waiting for transfers between devices: 120 us -> 0 us
  other arithmetic: 49.9 us -> 0 us
  blocking collectives: 40.9 us -> 0 us
  Pallas kernels: 0 us -> 37.2 us
  between operations: 14.3 us -> 0.67 us
  starting transfers between devices: 7.09 us -> 0 us
  matrix products: 6.65 us -> 0 us
  local copies, waits for them, and re-layouts: 9.83 us -> 4.1 us
    psum x1 -> x0, waiting for transfers between devices: 115 us -> none  [body(): gram = lax.psum(local_gram, ('gx', 'gz'))]
    psum x1 -> x0, blocking collectives: 40.9 us -> none  [body(): anchor = lax.psum(term, ('gx', 'gz'))]
    pallas_call x0 -> x2, Pallas kernels: none -> 37.2 us  [the longest x1 25.6 us: body(): pl.pallas_call(functools.partial(gram_kernel, dims), out_shape=(jax.Shape...]
    another operation x15 -> x0, other arithmetic: 36.2 us -> none  [the longest x9 19.6 us: orthonormal(): lower = jnp.linalg.cholesky(inner)]
    convert_element_type x1 -> x0, other arithmetic: 12.7 us -> none  [body(): flat = total.astype(jnp.bfloat16).reshape(snaps, planes * cols_x * cols_z)]
    ppermute x4 -> x0, starting transfers between devices: 7.05 us -> none  [the longest x2 6.99 us: extended(): lax.ppermute(head, axis, [((i + 1) % count, i) for i in range(count)])]
    dot_general x8 -> x0, matrix products: 5.9 us -> none  [the longest x3 3.45 us: body(): jnp.dot(weighted, basis_now, precision=lax.Precision.HIGHEST)]
    ppermute x4 -> x0, waiting for transfers between devices: 5.63 us -> none  [the longest x2 4.16 us: extended(): lax.ppermute(tail, axis, [(i, (i + 1) % count) for i in range(count)])]
  transfers between devices with their start and end apart: 5 -> 0, of which waited for: 3 -> 0; matrix products, arithmetic and copies ran while one was open for 1% -> 0% of each run, Pallas kernels for 0% -> 0%
where the time goes in v1:
time: 42.2 us; the launch traced here: 41.9 us
  Pallas kernels  37.2 us (88%)
  local copies, waits for them, and re-layouts  4.1 us (10%)
  between operations  0.67 us (2%)
    pallas_call x1, Pallas kernels, body(): pl.pallas_call(functools.partial(gram_kernel, dims), out_shape=(jax.Shape...  25.6 us
    pallas_call x1, Pallas kernels, body(): pl.pallas_call(functools.partial(modes_kernel, dims), out_shape=(jax.Shap...  11.6 us
    unnamed x8, local copies, waits for them, and re-layouts  4.1 us

profile of v1, /device:TPU:0, one launch (start us, length us, event | category | flops | bytes accessed | tf_op | source)
XLA Modules:
  0.0 41.9 jit_solution(13834276228102760153)
XLA Ops:
  0.6 0.0 copy-start.1
  0.6 0.9 %copy.6.start_ref = f32[128,64]{1,0:T(8,128)S(1)} copy(f32[128,64]{0,1:T(8,128)} %param.7) | data formatting | bytes 65536 | tf_op args[3]
  1.5 0.0 copy-start
  1.5 1.9 %copy-done = bf16[2,128,2,24,128]{4,3,2,1,0:T(8,128)(2,1)S(1)} copy-done((bf16[2,128,2,24,128]{4,3,2,1,0:T(8,128)(2,1)S(1)}, bf16[2,128,2,24,128]{4,3,2,1,0:T(8,128)(2,1)}, u32[]{:S(2)}) %copy-start) | copy-done | bytes 3145752
  3.4 0.0 copy-start.2
  3.4 0.7 %copy-done.2 = s32[64]{0:T(128)S(1)} copy-done((s32[64]{0:T(128)S(1)}, s32[64]{0:T(128)}, u32[]{:S(2)}) %copy-start.2) | copy-done | bytes 280
  4.0 25.6 %vorticity_gram.1 = (bf16[128,6144]{1,0:T(8,128)(2,1)S(1)}, f32[192,128]{1,0:T(8,128)S(1)}) custom-call(bf16[2,6144,128]{2,1,0:T(8,128)(2,1)S(1)} %bitcast.4, s32[1,64]{1,0:T(1,128)S(1)} %bitcast.6), custom_call_target="tpu_custom_call" | custom-call | tf_op jit(solution)/shard_map/vorticity_gram/pallas_call | solution.py:279
  29.6 0.0 copy-done.1
  29.6 11.6 %subspace_modes.1 = (bf16[3072,128]{1,0:T(8,128)(2,1)}, f32[128,64]{1,0:T(8,128)S(1)}) custom-call(f32[192,128]{1,0:T(8,128)S(1)} %get-tuple-element.6.gram_ref, bf16[128,6144]{1,0:T(8,128)(2,1)S(1)} %get-tuple-element.7.flat_ref, s32[1,128]{1,0:T(1,128)S(1)} %bitcast.5, f32[128,64]{1,0:T(8,128)S(1)} %copy.6.start_ref), custom_call_target="tpu_custom_call" | custom-call | tf_op jit(solution)/shard_map/subspace_modes/pallas_call | solution.py:309
  41.2 0.7 %copy.7 = f32[128,64]{0,1:T(8,128)} copy(f32[128,64]{1,0:T(8,128)S(1)} %get-tuple-element.11) | data formatting | bytes 65536
Async XLA Ops:
  0.6 29.0 %copy-start.1 = (s32[128]{0:T(128)S(1)}, s32[128]{0:T(128)}, u32[]{:S(2)}) copy-start(s32[128]{0:T(128)} %param.5) | copy-start | bytes 1540
  1.5 1.9 %copy-start = (bf16[2,128,2,24,128]{4,3,2,1,0:T(8,128)(2,1)S(1)}, bf16[2,128,2,24,128]{4,3,2,1,0:T(8,128)(2,1)}, u32[]{:S(2)}) copy-start(bf16[2,128,2,24,128]{4,3,2,1,0:T(8,128)(2,1)} %param.4) | copy-start | bytes 9437188
  3.4 0.7 %copy-start.2 = (s32[64]{0:T(128)S(1)}, s32[64]{0:T(128)}, u32[]{:S(2)}) copy-start(s32[64]{0:T(128)} %param.6) | copy-start | bytes 772

commit v2 on v1

--- a/solution.py
+++ b/solution.py
@@ -25,9 +25,9 @@
 
 
 def gram_kernel(
-    dims, vel_ref, anchor_ref, flat_ref, out_ref,
-    wide, uterm, sendx, recvx, sendz, recvz, part, got1, got2, got3,
-    sx_sem, rx_sem, sz_sem, rz_sem, s1_sem, r1_sem, s2_sem, r2_sem, s3_sem, r3_sem, s4_sem, r4_sem,
+    dims, vel_ref, anchor_ref, kept_ref, out_ref,
+    flat_ref, spans, streams, spots, wide, uterm, sendx, recvx, sendz, recvz, part, got1, got2, got3,
+    sx_sem, rx_sem, sz_sem, rz_sem, s1_sem, r1_sem, s2_sem, r2_sem, s3_sem, r3_sem, s4_sem, r4_sem, load_sem,
 ):
     snaps, planes, cx, cz, kept, nx, nz, group = dims
     rows = snaps * planes * cx
@@ -49,9 +49,20 @@
     if teams > 1:
         greet = greet + [(xnext, me_z), (xprev, me_z)]
 
+    quarter = rows // 4
+    loads = []
+    for half, kept_in in ((0, spans), (1, streams)):
+        for c in range(4):
+            here = pl.ds(c * quarter, quarter)
+            loads.append(pltpu.make_async_copy(
+                vel_ref.at[half, here], kept_in.at[here], load_sem.at[half * 4 + c]
+            ))
+    loads.append(pltpu.make_async_copy(anchor_ref, spots, load_sem.at[8]))
     barrier = pltpu.get_barrier_semaphore()
     for peer in greet:
         pl.semaphore_signal(barrier, inc=1, device_id=peer, device_id_type=MESH)
+    for copy in loads:
+        copy.start()
 
     def remote(src, dst, send, recv, peer):
         return pltpu.make_async_remote_copy(
@@ -59,7 +70,6 @@
             device_id=peer, device_id_type=MESH,
         )
 
-    quarter = rows // 4
     edge = iota((32, cz), 0)
     lane = iota((32, cz), 1)
     packed = jnp.zeros((32, quarter), F32)
@@ -67,19 +77,11 @@
         r = edge % 16 - 4 * c
         wanted = jnp.where(edge < 16, cz - REACH + r, r)
         pick = jnp.where((r >= 0) & (r < REACH) & (lane == wanted), 1.0, 0.0).astype(BF16)
+        loads[c].wait()
         packed = packed + lax.dot_general(
-            pick, vel_ref[0, c * quarter : (c + 1) * quarter, :], NT, preferred_element_type=F32
+            pick, spans[c * quarter : (c + 1) * quarter, :], NT, preferred_element_type=F32
         )
     sendz[...] = packed.astype(BF16).reshape(2, 16, quarter)
-
-    wide[...] = vel_ref[1].astype(F32)
-    for p in range(planes):
-        for r in range(REACH):
-            low = wide[pl.ds(p * cx + r, snaps, stride=stride), :]
-            high = wide[pl.ds(p * cx + cx - REACH + r, snaps, stride=stride), :]
-            sendx[0, p * REACH + r] = high.astype(BF16)
-            sendx[1, p * REACH + r] = low.astype(BF16)
-
     pl.semaphore_wait(barrier, len(greet))
     halos = [
         remote(sendz.at[0], recvz.at[0], sz_sem.at[0], rz_sem.at[0], (me_x, znext)),
@@ -87,10 +89,26 @@
         remote(sendx.at[0], recvx.at[0], sx_sem.at[0], rx_sem.at[0], (xnext, me_z)),
         remote(sendx.at[1], recvx.at[1], sx_sem.at[1], rx_sem.at[1], (xprev, me_z)),
     ]
-    for copy in halos:
-        copy.start()
-
-    index = anchor_ref[...]
+    halos[0].start()
+    halos[1].start()
+
+    some = snaps // 4
+    for c in range(4):
+        loads[4 + c].wait()
+        here = slice(c * quarter, (c + 1) * quarter)
+        wide[here, :] = streams[here, :].astype(F32)
+        for p in range(planes):
+            for r in range(REACH):
+                low = c * quarter + p * cx + r
+                block = wide[pl.ds(low + cx - REACH, some, stride=stride), :]
+                sendx[0, p * REACH + r, c * some : (c + 1) * some, :] = block.astype(BF16)
+                block = wide[pl.ds(low, some, stride=stride), :]
+                sendx[1, p * REACH + r, c * some : (c + 1) * some, :] = block.astype(BF16)
+    halos[2].start()
+    halos[3].start()
+
+    loads[8].wait()
+    index = spots[...]
     total_x, total_z = cx * nx, cz * nz
     plane_of = index // (total_x * total_z)
     remain = index % (total_x * total_z)
@@ -111,48 +129,53 @@
         spread = stencil_weight(jnp.where(valid, lane - source, 0))
         here = slice(c * quarter, (c + 1) * quarter)
         uterm[here, :] = jnp.dot(
-            vel_ref[0, here, :], band, preferred_element_type=F32
+            spans[here, :], band, preferred_element_type=F32
         ) + jnp.dot(sides, spread, preferred_element_type=F32)
+
+    def snapshots(begin, end):
+        def some_rows(step, carry):
+            first = pl.multiple_of(step * 16, 16)
+            for p in range(planes):
+                layers = {}
+                for x in range(begin - REACH, end + REACH):
+                    if x < 0:
+                        block = recvx[0, p * REACH + x + REACH, pl.ds(first, 16), :].astype(F32)
+                    elif x >= cx:
+                        block = recvx[1, p * REACH + x - cx, pl.ds(first, 16), :].astype(F32)
+                    else:
+                        block = wide[pl.ds(first * stride + p * cx + x, 16, stride=stride), :]
+                    layers[x] = block
+                for x in range(begin, end):
+                    value = 45.0 * (layers[x + 1] - layers[x - 1])
+                    value = value - 9.0 * (layers[x + 2] - layers[x - 2])
+                    value = value + (layers[x + 3] - layers[x - 3])
+                    value = value + uterm[pl.ds(first * stride + p * cx + x, 16, stride=stride), :]
+                    cell = (p * cx + x) * cz
+                    flat_ref[pl.ds(first, 16), cell : cell + cz] = (value * (1.0 / 60.0)).astype(BF16)
+            return carry
+
+        lax.fori_loop(0, snaps // 16, some_rows, 0)
+
+    def products(begin, end):
+        total = jnp.zeros((snaps + kept, snaps), F32)
+        for p in range(planes):
+            cell, width = (p * cx + begin) * cz, (end - begin) * cz
+            block = flat_ref[:, cell : cell + width]
+            cell_in = iota((kept, width), 1).astype(F32) + float(cell)
+            mark = jnp.where(cell_in == column, 1.0, 0.0).astype(BF16)
+            both = jnp.concatenate([block, mark], axis=0)
+            total = total + lax.dot_general(both, block, NT, preferred_element_type=F32)
+        return total
+
+    snapshots(REACH, cx - REACH)
+    part[...] = products(REACH, cx - REACH)
     halos[2].wait_recv()
     halos[3].wait_recv()
-
-    def snapshots(step, carry):
-        first = pl.multiple_of(step * 16, 16)
-        for p in range(planes):
-            layers = []
-            for x in range(-REACH, cx + REACH):
-                if x < 0:
-                    block = recvx[0, p * REACH + x + REACH, pl.ds(first, 16), :].astype(F32)
-                elif x >= cx:
-                    block = recvx[1, p * REACH + x - cx, pl.ds(first, 16), :].astype(F32)
-                else:
-                    block = wide[pl.ds(first * stride + p * cx + x, 16, stride=stride), :]
-                layers.append(block)
-            for x in range(cx):
-                at = x + REACH
-                value = 45.0 * (layers[at + 1] - layers[at - 1])
-                value = value - 9.0 * (layers[at + 2] - layers[at - 2])
-                value = value + (layers[at + 3] - layers[at - 3])
-                value = value + uterm[pl.ds(first * stride + p * cx + x, 16, stride=stride), :]
-                cell = (p * cx + x) * cz
-                flat_ref[pl.ds(first, 16), cell : cell + cz] = (value * (1.0 / 60.0)).astype(BF16)
-        return carry
-
-    lax.fori_loop(0, snaps // 16, snapshots, 0)
-
-    width = 8 * cz
-    cell_in = iota((kept, width), 1).astype(F32)
-
-    def products(step, total):
-        at = pl.multiple_of(step * width, width)
-        block = flat_ref[:, pl.ds(at, width)]
-        mark = jnp.where(cell_in + (step * width).astype(F32) == column, 1.0, 0.0).astype(BF16)
-        both = jnp.concatenate([block, mark], axis=0)
-        return total + lax.dot_general(both, block, NT, preferred_element_type=F32)
-
-    part[...] = lax.fori_loop(
-        0, planes * cx * cz // width, products, jnp.zeros((snaps + kept, snaps), F32)
-    )
+    snapshots(0, REACH)
+    snapshots(cx - REACH, cx)
+    store = pltpu.make_async_copy(flat_ref, kept_ref, load_sem.at[9])
+    store.start()
+    part[...] += products(0, REACH) + products(cx - REACH, cx)
 
     started = list(halos)
     first_stage = []
@@ -201,6 +224,7 @@
         copy.wait_recv()
     for copy in started + first_stage + last_stage:
         copy.wait_send()
+    store.wait()
 
 
 def orthonormal_rows(block, pivots):
@@ -213,33 +237,45 @@
     right = [block[8 * h : 8 * h + 8, :] for h in range(groups)]
     row_in = iota((8, snaps), 0)
     for k0 in range(0, kept, pivots):
-        g = k0 // 8
+        g, s0 = k0 // 8, k0 % 8
+        ahead = range(pivots)
         cols = [
-            {h: jnp.broadcast_to(left[h][:, k0 + j : k0 + j + 1], (8, snaps)) for h in range(g, groups)}
-            for j in range(pivots)
+            [None] * g
+            + [jnp.broadcast_to(left[h][:, k0 + n : k0 + n + 1], (8, snaps)) for h in range(g, groups)]
+            for n in ahead
         ]
-        for j in range(pivots):
-            s = (k0 + j) % 8
-            pivot = jnp.broadcast_to(cols[j][g][s : s + 1, :], (8, snaps))
+        own = [
+            [jnp.broadcast_to(cols[n][g][s0 + j : s0 + j + 1, :], (8, snaps)) for n in ahead]
+            for j in ahead
+        ]
+        lrow = [jnp.broadcast_to(left[g][s0 + j : s0 + j + 1, :], (8, kept)) for j in ahead]
+        rrow = [jnp.broadcast_to(right[g][s0 + j : s0 + j + 1, :], (8, snaps)) for j in ahead]
+        for j in ahead:
+            pivot = own[j][j]
             inverse = 1.0 / pivot
-            root = inverse * jnp.sqrt(pivot)
-            ahead = [cols[n][g][s : s + 1, :] * inverse for n in range(j + 1, pivots)]
-            left_row = left[g][s : s + 1, :] * inverse[:, :kept]
-            right_row = right[g][s : s + 1, :] * inverse
+            for n in range(j + 1, pivots):
+                for m in range(n, pivots):
+                    own[n][m] = own[n][m] - (own[j][n] * own[j][m]) * inverse
+            for n in range(j + 1, pivots):
+                times = own[j][n] * inverse
+                lrow[n] = lrow[n] - times[:, :kept] * lrow[j]
+                rrow[n] = rrow[n] - times * rrow[j]
+                for h in range(g, groups):
+                    cols[n][h] = cols[n][h] - times * cols[j][h]
             for h in range(g, groups):
-                factor = cols[j][h]
+                factor = cols[j][h] * inverse
                 if h == g:
-                    factor = jnp.where(row_in > s, factor, 0.0)
-                left[h] = left[h] - factor[:, :kept] * left_row
-                right[h] = right[h] - factor * right_row
-                for n in range(j + 1, pivots):
-                    cols[n][h] = cols[n][h] - factor * ahead[n - j - 1]
-            right[g] = jnp.where(row_in == s, right[g] * root, right[g])
+                    factor = jnp.where(row_in > s0 + j, factor, 0.0)
+                left[h] = left[h] - factor[:, :kept] * lrow[j]
+                right[h] = right[h] - factor * rrow[j]
+            right[g] = jnp.where(row_in == s0 + j, rrow[j] * (inverse * jnp.sqrt(pivot)), right[g])
     return jnp.concatenate(right, axis=0)
 
 
-def modes_kernel(dims, gram_ref, flat_ref, rank_ref, start_ref, modes_ref, basis_ref, spread):
+def modes_kernel(dims, gram_ref, kept_ref, rank_ref, start_ref, modes_ref, basis_ref, flat_ref, spread, sem):
     snaps, planes, cx, cz, kept, nx, nz, group = dims
+    fetch = pltpu.make_async_copy(kept_ref, flat_ref, sem)
+    fetch.start()
     cells = float(planes * cx * nx * cz * nz)
     stride = planes * cx
     scale = jnp.where(rank_ref[...] < kept, 1.0, 0.25).astype(F32)
@@ -252,16 +288,18 @@
         )
         return orthonormal_rows(moved, 4)
 
-    rows = lax.fori_loop(0, ITERS, iterate, jnp.transpose(start_ref[...]))
+    rows = lax.fori_loop(0, ITERS, iterate, start_ref[...])
     coef = (scale * rows).astype(BF16)
     anchor = jnp.sum(gram_ref[snaps : snaps + kept, :] * coef.astype(F32), axis=1, keepdims=True)
     orient = anchor / jnp.maximum(jnp.abs(anchor), 1.0)
-    basis_ref[...] = jnp.transpose(rows * orient)
-    for block in range(stride):
-        raw = jnp.dot(
-            coef, flat_ref[:, block * cz : (block + 1) * cz], preferred_element_type=F32
+    basis_ref[...] = rows * orient
+    fetch.wait()
+    for first in range(0, stride, 4):
+        raw = orient * jnp.dot(
+            coef, flat_ref[:, first * cz : (first + 4) * cz], preferred_element_type=F32
         )
-        spread[pl.ds(block, kept, stride=stride), :] = raw * orient
+        for n in range(4):
+            spread[pl.ds(first + n, kept, stride=stride), :] = raw[:, n * cz : (n + 1) * cz]
     modes_ref[...] = spread[...].astype(BF16)
 
 
@@ -275,6 +313,7 @@
     share = total // group
     teams = nx // group
     vmem = pl.BlockSpec(memory_space=pltpu.VMEM)
+    hbm = pl.BlockSpec(memory_space=pltpu.HBM)
     dma = lambda n: pltpu.SemaphoreType.DMA((max(n, 1),))
     flat, gram = pl.pallas_call(
         functools.partial(gram_kernel, dims),
@@ -282,9 +321,13 @@
             jax.ShapeDtypeStruct((snaps, planes * cx * cz), BF16),
             jax.ShapeDtypeStruct((total, snaps), F32),
         ),
-        in_specs=[vmem] * 2,
-        out_specs=(vmem, vmem),
+        in_specs=[hbm] * 2,
+        out_specs=(hbm, vmem),
         scratch_shapes=[
+            pltpu.VMEM((snaps, planes * cx * cz), BF16),
+            pltpu.VMEM((rows, cz), BF16),
+            pltpu.VMEM((rows, cz), BF16),
+            pltpu.VMEM((1, kept), jnp.int32),
             pltpu.VMEM((rows, cz), F32),
             pltpu.VMEM((rows, cz), F32),
             pltpu.VMEM((2, planes * REACH, snaps, cz), BF16),
@@ -299,10 +342,10 @@
             dma(group - 1), dma(group - 1),
             dma(nz - 1), dma(nz - 1),
             dma(group - 1), dma(group - 1),
-            dma(teams - 1), dma(teams - 1),
+            dma(teams - 1), dma(teams - 1), dma(10),
         ],
         compiler_params=pltpu.CompilerParams(
-            collective_id=0, has_side_effects=True, vmem_limit_bytes=40 * 1024 * 1024
+            collective_id=0, has_side_effects=True, vmem_limit_bytes=58 * 1024 * 1024
         ),
         name="vorticity_gram",
     )(velocity.reshape(2, rows, cz), anchor_index.reshape(1, kept))
@@ -310,15 +353,19 @@
         functools.partial(modes_kernel, dims),
         out_shape=(
             jax.ShapeDtypeStruct((kept * planes * cx, cz), BF16),
-            jax.ShapeDtypeStruct((snaps, kept), F32),
+            jax.ShapeDtypeStruct((kept, snaps), F32),
         ),
-        in_specs=[vmem] * 4,
+        in_specs=[vmem, hbm, vmem, vmem],
         out_specs=(vmem, vmem),
-        scratch_shapes=[pltpu.VMEM((kept * planes * cx, cz), F32)],
-        compiler_params=pltpu.CompilerParams(vmem_limit_bytes=40 * 1024 * 1024),
+        scratch_shapes=[
+            pltpu.VMEM((snaps, planes * cx * cz), BF16),
+            pltpu.VMEM((kept * planes * cx, cz), F32),
+            pltpu.SemaphoreType.DMA,
+        ],
+        compiler_params=pltpu.CompilerParams(vmem_limit_bytes=58 * 1024 * 1024),
         name="subspace_modes",
-    )(gram, flat, snapshot_rank.reshape(1, snaps), start_basis)
-    return modes.reshape(kept, planes, cx, cz), basis
+    )(gram, flat, snapshot_rank.reshape(1, snaps), start_basis.T)
+    return modes.reshape(kept, planes, cx, cz), basis.T
 
 
 def solution(mesh):

time: 42.2 us -> 39.9 us (0.945)
  local copies, waits for them, and re-layouts: 4.1 us -> 0 us
  Pallas kernels: 37.2 us -> 39.1 us
    unnamed x8 -> x0, local copies, waits for them, and re-layouts: 4.1 us -> none
    pallas_call x1, Pallas kernels: 25.6 us -> 26.9 us  [body(): pl.pallas_call(functools.partial(gram_kernel, dims), out_shape=(jax.Shape...]
    pallas_call x1, Pallas kernels: 11.6 us -> 12.2 us  [body(): pl.pallas_call(functools.partial(modes_kernel, dims), out_shape=(jax.Shap...]
where the time goes in v2:
time: 39.9 us; the launch traced here: 39.7 us
  Pallas kernels  39.1 us (98%)
  between operations  0.64 us (2%)
    pallas_call x1, Pallas kernels, body(): pl.pallas_call(functools.partial(gram_kernel, dims), out_shape=(jax.Shape...  26.9 us
    pallas_call x1, Pallas kernels, body(): pl.pallas_call(functools.partial(modes_kernel, dims), out_shape=(jax.Shap...  12.2 us

profile of v2, /device:TPU:0, one launch (start us, length us, event | category | flops | bytes accessed | tf_op | source)
XLA Modules:
  0.0 39.7 jit_solution(11795206133048067338)
XLA Ops:
  0.6 26.9 %vorticity_gram.1 = (bf16[128,6144]{1,0:T(8,128)(2,1)}, f32[192,128]{1,0:T(8,128)}) custom-call(bf16[2,6144,128]{2,1,0:T(8,128)(2,1)} %bitcast.6, s32[1,64]{1,0:T(1,128)} %bitcast.9), custom_call_target="tpu_custom_call" | custom-call | tf_op jit(solution)/shard_map/vorticity_gram/pallas_call | solution.py:318
  27.5 12.2 %subspace_modes.1 = (bf16[3072,128]{1,0:T(8,128)(2,1)}, f32[64,128]{1,0:T(8,128)}) custom-call(f32[192,128]{1,0:T(8,128)} %get-tuple-element.6.gram_ref, bf16[128,6144]{1,0:T(8,128)(2,1)} %get-tuple-element.7.kept_ref, s32[1,128]{1,0:T(1,128)} %bitcast.8, f32[64,128]{1,0:T(8,128)} %bitcast.7), custom_call_target="tpu_custom_call" | custom-call | tf_op jit(solution)/shard_map/subspace_modes/pallas_call | solution.py:352

commit v3 on v2

--- a/solution.py
+++ b/solution.py
@@ -32,6 +32,7 @@
     snaps, planes, cx, cz, kept, nx, nz, group = dims
     rows = snaps * planes * cx
     stride = planes * cx
+    pitch = stride + 1
     me_x = lax.axis_index("gx")
     me_z = lax.axis_index("gz")
     member = lax.rem(me_x, group)
@@ -95,14 +96,19 @@
     some = snaps // 4
     for c in range(4):
         loads[4 + c].wait()
-        here = slice(c * quarter, (c + 1) * quarter)
-        wide[here, :] = streams[here, :].astype(F32)
+
+        def widen(m, carry, first=c * some):
+            at = pl.multiple_of((first + m) * stride, 16)
+            wide[pl.ds((first + m) * pitch, stride), :] = streams[pl.ds(at, stride), :].astype(F32)
+            return carry
+
+        lax.fori_loop(0, some, widen, 0, unroll=8)
         for p in range(planes):
             for r in range(REACH):
-                low = c * quarter + p * cx + r
-                block = wide[pl.ds(low + cx - REACH, some, stride=stride), :]
+                low = c * some * pitch + p * cx + r
+                block = wide[pl.ds(low + cx - REACH, some, stride=pitch), :]
                 sendx[0, p * REACH + r, c * some : (c + 1) * some, :] = block.astype(BF16)
-                block = wide[pl.ds(low, some, stride=stride), :]
+                block = wide[pl.ds(low, some, stride=pitch), :]
                 sendx[1, p * REACH + r, c * some : (c + 1) * some, :] = block.astype(BF16)
     halos[2].start()
     halos[3].start()
@@ -122,15 +128,22 @@
     halos[0].wait_recv()
     halos[1].wait_recv()
     sides = jnp.transpose(recvz[...].reshape(32, quarter).astype(F32)).astype(BF16)
-    for c in range(4):
+
+    def spanwise(c, carry):
         r = edge % 16 - 4 * c
         source = jnp.where(edge < 16, r - REACH, cz + r)
         valid = (r >= 0) & (r < REACH)
         spread = stencil_weight(jnp.where(valid, lane - source, 0))
-        here = slice(c * quarter, (c + 1) * quarter)
-        uterm[here, :] = jnp.dot(
+        here = pl.ds(pl.multiple_of(c * quarter, 16), quarter)
+        value = jnp.dot(
             spans[here, :], band, preferred_element_type=F32
         ) + jnp.dot(sides, spread, preferred_element_type=F32)
+        for m in range(some):
+            at = pl.ds((c * some + m) * pitch, stride)
+            uterm[at, :] = value[m * stride : (m + 1) * stride, :]
+        return carry
+
+    lax.fori_loop(0, 4, spanwise, 0)
 
     def snapshots(begin, end):
         def some_rows(step, carry):
@@ -143,13 +156,13 @@
                     elif x >= cx:
                         block = recvx[1, p * REACH + x - cx, pl.ds(first, 16), :].astype(F32)
                     else:
-                        block = wide[pl.ds(first * stride + p * cx + x, 16, stride=stride), :]
+                        block = wide[pl.ds(first * pitch + p * cx + x, 16, stride=pitch), :]
                     layers[x] = block
                 for x in range(begin, end):
                     value = 45.0 * (layers[x + 1] - layers[x - 1])
                     value = value - 9.0 * (layers[x + 2] - layers[x - 2])
                     value = value + (layers[x + 3] - layers[x - 3])
-                    value = value + uterm[pl.ds(first * stride + p * cx + x, 16, stride=stride), :]
+                    value = value + uterm[pl.ds(first * pitch + p * cx + x, 16, stride=pitch), :]
                     cell = (p * cx + x) * cz
                     flat_ref[pl.ds(first, 16), cell : cell + cz] = (value * (1.0 / 60.0)).astype(BF16)
             return carry
@@ -299,8 +312,14 @@
             coef, flat_ref[:, first * cz : (first + 4) * cz], preferred_element_type=F32
         )
         for n in range(4):
-            spread[pl.ds(first + n, kept, stride=stride), :] = raw[:, n * cz : (n + 1) * cz]
-    modes_ref[...] = spread[...].astype(BF16)
+            spread[pl.ds(first + n, kept, stride=stride + 1), :] = raw[:, n * cz : (n + 1) * cz]
+
+    def narrow(k, carry):
+        block = spread[pl.ds(k * (stride + 1), stride), :]
+        modes_ref[pl.ds(pl.multiple_of(k * stride, 16), stride), :] = block.astype(BF16)
+        return carry
+
+    lax.fori_loop(0, kept, narrow, 0, unroll=8)
 
 
 def body(nx, nz, velocity, snapshot_rank, anchor_index, start_basis):
@@ -328,8 +347,8 @@
             pltpu.VMEM((rows, cz), BF16),
             pltpu.VMEM((rows, cz), BF16),
             pltpu.VMEM((1, kept), jnp.int32),
-            pltpu.VMEM((rows, cz), F32),
-            pltpu.VMEM((rows, cz), F32),
+            pltpu.VMEM((rows + snaps, cz), F32),
+            pltpu.VMEM((rows + snaps, cz), F32),
             pltpu.VMEM((2, planes * REACH, snaps, cz), BF16),
             pltpu.VMEM((2, planes * REACH, snaps, cz), BF16),
             pltpu.VMEM((2, 16, rows // 4), BF16),
@@ -359,7 +378,7 @@
         out_specs=(vmem, vmem),
         scratch_shapes=[
             pltpu.VMEM((snaps, planes * cx * cz), BF16),
-            pltpu.VMEM((kept * planes * cx, cz), F32),
+            pltpu.VMEM((kept * (planes * cx + 1), cz), F32),
             pltpu.SemaphoreType.DMA,
         ],
         compiler_params=pltpu.CompilerParams(vmem_limit_bytes=58 * 1024 * 1024),

time: 39.9 us -> 38.2 us (0.957)
  Pallas kernels: 39.1 us -> 37.4 us
    pallas_call x1, Pallas kernels: 26.9 us -> 25.4 us  [body(): pl.pallas_call(functools.partial(gram_kernel, dims), out_shape=(jax.Shape...]
where the time goes in v3:
time: 38.2 us; the launch traced here: 38 us
  Pallas kernels  37.4 us (98%)
  between operations  0.64 us (2%)
    pallas_call x1, Pallas kernels, body(): pl.pallas_call(functools.partial(gram_kernel, dims), out_shape=(jax.Shape...  25.4 us
    pallas_call x1, Pallas kernels, body(): pl.pallas_call(functools.partial(modes_kernel, dims), out_shape=(jax.Shap...  12 us

profile of v3, /device:TPU:0, one launch (start us, length us, event | category | flops | bytes accessed | tf_op | source)
XLA Modules:
  0.0 38.0 jit_solution(3504269712112176257)
XLA Ops:
  0.6 25.4 %vorticity_gram.1 = (bf16[128,6144]{1,0:T(8,128)(2,1)}, f32[192,128]{1,0:T(8,128)}) custom-call(bf16[2,6144,128]{2,1,0:T(8,128)(2,1)} %bitcast.6, s32[1,64]{1,0:T(1,128)} %bitcast.9), custom_call_target="tpu_custom_call" | custom-call | tf_op jit(solution)/shard_map/vorticity_gram/pallas_call | solution.py:337
  26.0 12.0 %subspace_modes.1 = (bf16[3072,128]{1,0:T(8,128)(2,1)}, f32[64,128]{1,0:T(8,128)}) custom-call(f32[192,128]{1,0:T(8,128)} %get-tuple-element.6.gram_ref, bf16[128,6144]{1,0:T(8,128)(2,1)} %get-tuple-element.7.kept_ref, s32[1,128]{1,0:T(1,128)} %bitcast.8, f32[64,128]{1,0:T(8,128)} %bitcast.7), custom_call_target="tpu_custom_call" | custom-call | tf_op jit(solution)/shard_map/subspace_modes/pallas_call | solution.py:371

commit v4 on v3

--- a/solution.py
+++ b/solution.py
@@ -265,7 +265,8 @@
         rrow = [jnp.broadcast_to(right[g][s0 + j : s0 + j + 1, :], (8, snaps)) for j in ahead]
         for j in ahead:
             pivot = own[j][j]
-            inverse = 1.0 / pivot
+            guess = pl.reciprocal(pivot, approx=True)
+            inverse = guess * (2.0 - pivot * guess)
             for n in range(j + 1, pivots):
                 for m in range(n, pivots):
                     own[n][m] = own[n][m] - (own[j][n] * own[j][m]) * inverse
@@ -285,7 +286,7 @@
     return jnp.concatenate(right, axis=0)
 
 
-def modes_kernel(dims, gram_ref, kept_ref, rank_ref, start_ref, modes_ref, basis_ref, flat_ref, spread, sem):
+def modes_kernel(dims, gram_ref, kept_ref, rank_ref, start_ref, modes_ref, basis_ref, flat_ref, spread, packed, sem, sems):
     snaps, planes, cx, cz, kept, nx, nz, group = dims
     fetch = pltpu.make_async_copy(kept_ref, flat_ref, sem)
     fetch.start()
@@ -316,10 +317,18 @@
 
     def narrow(k, carry):
         block = spread[pl.ds(k * (stride + 1), stride), :]
-        modes_ref[pl.ds(pl.multiple_of(k * stride, 16), stride), :] = block.astype(BF16)
+        packed[pl.ds(pl.multiple_of(k * stride, 16), stride), :] = block.astype(BF16)
         return carry
 
-    lax.fori_loop(0, kept, narrow, 0, unroll=8)
+    part = kept // 4
+    writes = []
+    for n in range(4):
+        lax.fori_loop(n * part, (n + 1) * part, narrow, 0, unroll=True)
+        here = pl.ds(n * part * stride, part * stride)
+        writes.append(pltpu.make_async_copy(packed.at[here], modes_ref.at[here], sems.at[n]))
+        writes[-1].start()
+    for copy in writes:
+        copy.wait()
 
 
 def body(nx, nz, velocity, snapshot_rank, anchor_index, start_basis):
@@ -375,11 +384,13 @@
             jax.ShapeDtypeStruct((kept, snaps), F32),
         ),
         in_specs=[vmem, hbm, vmem, vmem],
-        out_specs=(vmem, vmem),
+        out_specs=(hbm, vmem),
         scratch_shapes=[
             pltpu.VMEM((snaps, planes * cx * cz), BF16),
             pltpu.VMEM((kept * (planes * cx + 1), cz), F32),
+            pltpu.VMEM((kept * planes * cx, cz), BF16),
             pltpu.SemaphoreType.DMA,
+            dma(4),
         ],
         compiler_params=pltpu.CompilerParams(vmem_limit_bytes=58 * 1024 * 1024),
         name="subspace_modes",

time: 38.2 us -> 39.2 us (1.026)
  Pallas kernels: 37.4 us -> 38.4 us
    pallas_call x1, Pallas kernels: 12 us -> 13 us  [body(): pl.pallas_call(functools.partial(modes_kernel, dims), out_shape=(jax.Shap...]
where the time goes in v4:
time: 39.2 us; the launch traced here: 39.1 us
  Pallas kernels  38.4 us (98%)
  between operations  0.64 us (2%)
    pallas_call x1, Pallas kernels, body(): pl.pallas_call(functools.partial(gram_kernel, dims), out_shape=(jax.Shape...  25.4 us
    pallas_call x1, Pallas kernels, body(): pl.pallas_call(functools.partial(modes_kernel, dims), out_shape=(jax.Shap...  13 us

profile of v4, /device:TPU:0, one launch (start us, length us, event | category | flops | bytes accessed | tf_op | source)
XLA Modules:
  0.0 39.1 jit_solution(9021038630936963200)
XLA Ops:
  0.6 25.4 %vorticity_gram.1 = (bf16[128,6144]{1,0:T(8,128)(2,1)}, f32[192,128]{1,0:T(8,128)}) custom-call(bf16[2,6144,128]{2,1,0:T(8,128)(2,1)} %bitcast.6, s32[1,64]{1,0:T(1,128)} %bitcast.9), custom_call_target="tpu_custom_call" | custom-call | tf_op jit(solution)/shard_map/vorticity_gram/pallas_call | solution.py:346
  26.0 13.0 %subspace_modes.1 = (bf16[3072,128]{1,0:T(8,128)(2,1)}, f32[64,128]{1,0:T(8,128)}) custom-call(f32[192,128]{1,0:T(8,128)} %get-tuple-element.6.gram_ref, bf16[128,6144]{1,0:T(8,128)(2,1)} %get-tuple-element.7.kept_ref, s32[1,128]{1,0:T(1,128)} %bitcast.8, f32[64,128]{1,0:T(8,128)} %bitcast.7), custom_call_target="tpu_custom_call" | custom-call | tf_op jit(solution)/shard_map/subspace_modes/pallas_call | solution.py:380

commit v5 on v3

--- a/solution.py
+++ b/solution.py
@@ -62,7 +62,7 @@
     barrier = pltpu.get_barrier_semaphore()
     for peer in greet:
         pl.semaphore_signal(barrier, inc=1, device_id=peer, device_id_type=MESH)
-    for copy in loads:
+    for copy in loads[:4] + loads[8:]:
         copy.start()
 
     def remote(src, dst, send, recv, peer):
@@ -79,6 +79,7 @@
         wanted = jnp.where(edge < 16, cz - REACH + r, r)
         pick = jnp.where((r >= 0) & (r < REACH) & (lane == wanted), 1.0, 0.0).astype(BF16)
         loads[c].wait()
+        loads[4 + c].start()
         packed = packed + lax.dot_general(
             pick, spans[c * quarter : (c + 1) * quarter, :], NT, preferred_element_type=F32
         )
@@ -145,12 +146,13 @@
 
     lax.fori_loop(0, 4, spanwise, 0)
 
-    def snapshots(begin, end):
+    def snapshots(*spans_x):
         def some_rows(step, carry):
             first = pl.multiple_of(step * 16, 16)
             for p in range(planes):
                 layers = {}
-                for x in range(begin - REACH, end + REACH):
+                needed = {x + d for begin, end in spans_x for x in range(begin, end) for d in range(-REACH, REACH + 1)}
+                for x in sorted(needed):
                     if x < 0:
                         block = recvx[0, p * REACH + x + REACH, pl.ds(first, 16), :].astype(F32)
                     elif x >= cx:
@@ -158,7 +160,7 @@
                     else:
                         block = wide[pl.ds(first * pitch + p * cx + x, 16, stride=pitch), :]
                     layers[x] = block
-                for x in range(begin, end):
+                for x in [x for begin, end in spans_x for x in range(begin, end)]:
                     value = 45.0 * (layers[x + 1] - layers[x - 1])
                     value = value - 9.0 * (layers[x + 2] - layers[x - 2])
                     value = value + (layers[x + 3] - layers[x - 3])
@@ -180,12 +182,11 @@
             total = total + lax.dot_general(both, block, NT, preferred_element_type=F32)
         return total
 
-    snapshots(REACH, cx - REACH)
+    snapshots((REACH, cx - REACH))
     part[...] = products(REACH, cx - REACH)
     halos[2].wait_recv()
     halos[3].wait_recv()
-    snapshots(0, REACH)
-    snapshots(cx - REACH, cx)
+    snapshots((0, REACH), (cx - REACH, cx))
     store = pltpu.make_async_copy(flat_ref, kept_ref, load_sem.at[9])
     store.start()
     part[...] += products(0, REACH) + products(cx - REACH, cx)
@@ -299,7 +300,7 @@
         moved = lax.dot_general(
             rows, weighted, NT, precision=lax.Precision.HIGHEST, preferred_element_type=F32
         )
-        return orthonormal_rows(moved, 4)
+        return orthonormal_rows(moved, 8)
 
     rows = lax.fori_loop(0, ITERS, iterate, start_ref[...])
     coef = (scale * rows).astype(BF16)

time: 38.2 us -> 36 us (0.942)
  Pallas kernels: 37.4 us -> 35.2 us
    pallas_call x1, Pallas kernels: 12 us -> 9.86 us  [body(): pl.pallas_call(functools.partial(modes_kernel, dims), out_shape=(jax.Shap...]
where the time goes in v5:
time: 36 us; the launch traced here: 35.8 us
  Pallas kernels  35.2 us (98%)
  between operations  0.64 us (2%)
    pallas_call x1, Pallas kernels, body(): pl.pallas_call(functools.partial(gram_kernel, dims), out_shape=(jax.Shape...  25.3 us
    pallas_call x1, Pallas kernels, body(): pl.pallas_call(functools.partial(modes_kernel, dims), out_shape=(jax.Shap...  9.86 us

profile of v5, /device:TPU:0, one launch (start us, length us, event | category | flops | bytes accessed | tf_op | source)
XLA Modules:
  0.0 35.8 jit_solution(10850169366348335422)
XLA Ops:
  0.6 25.3 %vorticity_gram.1 = (bf16[128,6144]{1,0:T(8,128)(2,1)}, f32[192,128]{1,0:T(8,128)}) custom-call(bf16[2,6144,128]{2,1,0:T(8,128)(2,1)} %bitcast.6, s32[1,64]{1,0:T(1,128)} %bitcast.9), custom_call_target="tpu_custom_call" | custom-call | tf_op jit(solution)/shard_map/vorticity_gram/pallas_call | solution.py:338
  26.0 9.9 %subspace_modes.1 = (bf16[3072,128]{1,0:T(8,128)(2,1)}, f32[64,128]{1,0:T(8,128)}) custom-call(f32[192,128]{1,0:T(8,128)} %get-tuple-element.6.gram_ref, bf16[128,6144]{1,0:T(8,128)(2,1)} %get-tuple-element.7.kept_ref, s32[1,128]{1,0:T(1,128)} %bitcast.8, f32[64,128]{1,0:T(8,128)} %bitcast.7), custom_call_target="tpu_custom_call" | custom-call | tf_op jit(solution)/shard_map/subspace_modes/pallas_call | solution.py:372

commit v6 on v5

--- a/solution.py
+++ b/solution.py
@@ -241,7 +241,7 @@
     store.wait()
 
 
-def orthonormal_rows(block, pivots):
+def orthonormal_rows(block):
     kept, snaps = block.shape
     inner = lax.dot_general(
         block, block, NT, precision=lax.Precision.HIGHEST, preferred_element_type=F32
@@ -250,39 +250,48 @@
     left = [inner[8 * h : 8 * h + 8, :] for h in range(groups)]
     right = [block[8 * h : 8 * h + 8, :] for h in range(groups)]
     row_in = iota((8, snaps), 0)
-    for k0 in range(0, kept, pivots):
-        g, s0 = k0 // 8, k0 % 8
-        ahead = range(pivots)
+    eight = range(8)
+    for g in range(groups):
+        below = range(g + 1, groups)
         cols = [
-            [None] * g
-            + [jnp.broadcast_to(left[h][:, k0 + n : k0 + n + 1], (8, snaps)) for h in range(g, groups)]
-            for n in ahead
+            {h: jnp.broadcast_to(left[h][:, 8 * g + n : 8 * g + n + 1], (8, snaps)) for h in range(g, groups)}
+            for n in eight
         ]
         own = [
-            [jnp.broadcast_to(cols[n][g][s0 + j : s0 + j + 1, :], (8, snaps)) for n in ahead]
-            for j in ahead
+            [jnp.broadcast_to(cols[n][g][j : j + 1, :], (8, snaps)) for n in eight] for j in eight
         ]
-        lrow = [jnp.broadcast_to(left[g][s0 + j : s0 + j + 1, :], (8, kept)) for j in ahead]
-        rrow = [jnp.broadcast_to(right[g][s0 + j : s0 + j + 1, :], (8, snaps)) for j in ahead]
-        for j in ahead:
-            pivot = own[j][j]
-            inverse = 1.0 / pivot
-            for n in range(j + 1, pivots):
-                for m in range(n, pivots):
-                    own[n][m] = own[n][m] - (own[j][n] * own[j][m]) * inverse
-            for n in range(j + 1, pivots):
-                times = own[j][n] * inverse
-                lrow[n] = lrow[n] - times[:, :kept] * lrow[j]
-                rrow[n] = rrow[n] - times * rrow[j]
-                for h in range(g, groups):
-                    cols[n][h] = cols[n][h] - times * cols[j][h]
-            for h in range(g, groups):
-                factor = cols[j][h] * inverse
-                if h == g:
-                    factor = jnp.where(row_in > s0 + j, factor, 0.0)
-                left[h] = left[h] - factor[:, :kept] * lrow[j]
-                right[h] = right[h] - factor * rrow[j]
-            right[g] = jnp.where(row_in == s0 + j, rrow[j] * (inverse * jnp.sqrt(pivot)), right[g])
+        lrow = [jnp.broadcast_to(left[g][j : j + 1, :], (8, kept)) for j in eight]
+        rrow = [jnp.broadcast_to(right[g][j : j + 1, :], (8, snaps)) for j in eight]
+
+        def clear(j, n, times):
+            lrow[n] = lrow[n] - times[:, :kept] * lrow[j]
+            rrow[n] = rrow[n] - times * rrow[j]
+            for h in below:
+                cols[n][h] = cols[n][h] - times * cols[j][h]
+
+        for j in range(0, 8, 2):
+            first, cross = own[j][j], own[j][j + 1]
+            det = first * own[j + 1][j + 1] - cross * cross
+            one = 1.0 / first
+            two = first * (1.0 / det)
+            ratio = cross * one
+            for n in range(j + 2, 8):
+                own[j + 1][n] = own[j + 1][n] - ratio * own[j][n]
+            for n in range(j + 2, 8):
+                for m in range(n, 8):
+                    own[n][m] = own[n][m] - (own[j][n] * own[j][m]) * one
+                    own[n][m] = own[n][m] - (own[j + 1][n] * own[j + 1][m]) * two
+            clear(j, j + 1, ratio)
+            for n in range(j + 2, 8):
+                clear(j, n, own[j][n] * one)
+                clear(j + 1, n, own[j + 1][n] * two)
+            for i, inverse in ((j, one), (j + 1, two)):
+                for h in below:
+                    factor = cols[i][h] * inverse
+                    left[h] = left[h] - factor[:, :kept] * lrow[i]
+                    right[h] = right[h] - factor * rrow[i]
+                done = rrow[i] * jnp.sqrt(inverse)
+                right[g] = done if i == 0 else jnp.where(row_in == i, done, right[g])
     return jnp.concatenate(right, axis=0)
 
 
@@ -295,14 +304,18 @@
     scale = jnp.where(rank_ref[...] < kept, 1.0, 0.25).astype(F32)
     down = jnp.transpose(jnp.broadcast_to(scale, (snaps, snaps)))
     weighted = down * (gram_ref[0:snaps, :] / cells) * scale
+    diagonal = iota((snaps, snaps), 0) == iota((snaps, snaps), 1)
+    weighted = weighted / jnp.sum(jnp.where(diagonal, weighted, 0.0))
+    start = start_ref[...]
+    start = start / jnp.max(jnp.abs(start), axis=1, keepdims=True)
 
     def iterate(step, rows):
         moved = lax.dot_general(
             rows, weighted, NT, precision=lax.Precision.HIGHEST, preferred_element_type=F32
         )
-        return orthonormal_rows(moved, 8)
-
-    rows = lax.fori_loop(0, ITERS, iterate, start_ref[...])
+        return orthonormal_rows(moved)
+
+    rows = lax.fori_loop(0, ITERS, iterate, start)
     coef = (scale * rows).astype(BF16)
     anchor = jnp.sum(gram_ref[snaps : snaps + kept, :] * coef.astype(F32), axis=1, keepdims=True)
     orient = anchor / jnp.maximum(jnp.abs(anchor), 1.0)

time: 36 us -> 35.8 us (level)
  no operation moved by 1% of the time
where the time goes in v6:
time: 35.8 us; the launch traced here: 35.6 us
  Pallas kernels  35 us (98%)
  between operations  0.64 us (2%)
    pallas_call x1, Pallas kernels, body(): pl.pallas_call(functools.partial(gram_kernel, dims), out_shape=(jax.Shape...  25.3 us
    pallas_call x1, Pallas kernels, body(): pl.pallas_call(functools.partial(modes_kernel, dims), out_shape=(jax.Shap...  9.62 us

profile of v6, /device:TPU:0, one launch (start us, length us, event | category | flops | bytes accessed | tf_op | source)
XLA Modules:
  0.0 35.6 jit_solution(3878478302539280789)
XLA Ops:
  0.6 25.3 %vorticity_gram.1 = (bf16[128,6144]{1,0:T(8,128)(2,1)}, f32[192,128]{1,0:T(8,128)}) custom-call(bf16[2,6144,128]{2,1,0:T(8,128)(2,1)} %bitcast.6, s32[1,64]{1,0:T(1,128)} %bitcast.9), custom_call_target="tpu_custom_call" | custom-call | tf_op jit(solution)/shard_map/vorticity_gram/pallas_call | solution.py:351
  26.0 9.6 %subspace_modes.1 = (bf16[3072,128]{1,0:T(8,128)(2,1)}, f32[64,128]{1,0:T(8,128)}) custom-call(f32[192,128]{1,0:T(8,128)} %get-tuple-element.6.gram_ref, bf16[128,6144]{1,0:T(8,128)(2,1)} %get-tuple-element.7.kept_ref, s32[1,128]{1,0:T(1,128)} %bitcast.8, f32[64,128]{1,0:T(8,128)} %bitcast.7), custom_call_target="tpu_custom_call" | custom-call | tf_op jit(solution)/shard_map/subspace_modes/pallas_call | solution.py:385

commit v7 on v5

--- a/solution.py
+++ b/solution.py
@@ -274,12 +274,10 @@
                 times = own[j][n] * inverse
                 lrow[n] = lrow[n] - times[:, :kept] * lrow[j]
                 rrow[n] = rrow[n] - times * rrow[j]
-                for h in range(g, groups):
+                for h in range(g + 1, groups):
                     cols[n][h] = cols[n][h] - times * cols[j][h]
-            for h in range(g, groups):
+            for h in range(g + 1, groups):
                 factor = cols[j][h] * inverse
-                if h == g:
-                    factor = jnp.where(row_in > s0 + j, factor, 0.0)
                 left[h] = left[h] - factor[:, :kept] * lrow[j]
                 right[h] = right[h] - factor * rrow[j]
             right[g] = jnp.where(row_in == s0 + j, rrow[j] * (inverse * jnp.sqrt(pivot)), right[g])

time: 36 us -> 35.8 us (level)
  no operation moved by 1% of the time
where the time goes in v7:
time: 35.8 us; the launch traced here: 35.7 us
  Pallas kernels  35 us (98%)
  between operations  0.64 us (2%)
    pallas_call x1, Pallas kernels, body(): pl.pallas_call(functools.partial(gram_kernel, dims), out_shape=(jax.Shape...  25.3 us
    pallas_call x1, Pallas kernels, body(): pl.pallas_call(functools.partial(modes_kernel, dims), out_shape=(jax.Shap...  9.68 us

profile of v7, /device:TPU:0, one launch (start us, length us, event | category | flops | bytes accessed | tf_op | source)
XLA Modules:
  0.0 35.7 jit_solution(9030974883110306664)
XLA Ops:
  0.6 25.3 %vorticity_gram.1 = (bf16[128,6144]{1,0:T(8,128)(2,1)}, f32[192,128]{1,0:T(8,128)}) custom-call(bf16[2,6144,128]{2,1,0:T(8,128)(2,1)} %bitcast.6, s32[1,64]{1,0:T(1,128)} %bitcast.9), custom_call_target="tpu_custom_call" | custom-call | tf_op jit(solution)/shard_map/vorticity_gram/pallas_call | solution.py:336
  26.0 9.7 %subspace_modes.1 = (bf16[3072,128]{1,0:T(8,128)(2,1)}, f32[64,128]{1,0:T(8,128)}) custom-call(f32[192,128]{1,0:T(8,128)} %get-tuple-element.6.gram_ref, bf16[128,6144]{1,0:T(8,128)(2,1)} %get-tuple-element.7.kept_ref, s32[1,128]{1,0:T(1,128)} %bitcast.8, f32[64,128]{1,0:T(8,128)} %bitcast.7), custom_call_target="tpu_custom_call" | custom-call | tf_op jit(solution)/shard_map/subspace_modes/pallas_call | solution.py:370
